TPU v7x, 32 devices: a whole 2x2x4 slice. The times are simulated.
32 devices in a mesh: groups: 2 (over x), patch: 16 (over z, y, core).
Axes of the slice: x: 2, y: 2, z: 4, core: 2. Of those that a mesh axis runs over, the one named last changes fastest.
Arguments:
- latents: bfloat16 [2816, 1280], P(('groups', 'patch')), parts along dimension 0, may hold values from -45 to 45, as said below
- stale_kv: bfloat16 [2816, 1280], P(('groups', 'patch')), parts along dimension 0, may hold values from -120 to 120
- stale_moments: float32 [32, 64], P(('groups', 'patch')), parts along dimension 0, may hold values from -1760 to 140800, as said below
- norm_gain: float32 [1280], replicated, may hold values from 0.25 to 1.75
- norm_shift: float32 [1280], replicated, may hold values from -3 to 3
- w_qkv: bfloat16 [1280, 1920], replicated, may hold values from -0.3125 to 0.3125
- w_out: bfloat16 [640, 1280], replicated, may hold values from -0.25 to 0.25
- out_bias: float32 [1280], replicated, may hold values from -2 to 2
Outputs:
- attention_out: bfloat16 [2816, 1280], P(('groups', 'patch')), parts along dimension 0
- fresh_kv: bfloat16 [2816, 1280], P(('groups', 'patch')), parts along dimension 0
There are 2 independent parts, one for each index of `groups`. A program takes and returns all parts, laid end to end along the dimension named above; an argument that names none is the same for every part. Nothing has to cross between parts.
Inputs may be any that keep to these rules, and one draw needn't show every extreme that they name: `latents`: channels have scales of their own and tokens too. `stale_moments`: each row holds for every group the sum of values and the sum of their squares over 3520 elements.
All inputs are finite; a program needn't handle non-finite values.
Results may differ from a plain program's by a relative error of at most 0.0065.
The roundings to bfloat16 on the way count: a program that leaves them out, or rounds other values in their place, can miss the bound.
Values may be sent and summed in bfloat16 or wider, within the bound.
A program may use at most 128 MiB of HBM per device.

v0:
```python
import math

import jax
import jax.numpy as jnp
from jax import lax
from jax.sharding import PartitionSpec as P

HDIM = 64


def absorb(state, queries, key_piece, piece_start, own_start, own_count):
    running_max, total_mass, weighted = state
    head_count = queries.shape[1]
    head_width = queries.shape[2]
    inner_width = head_count * head_width
    piece_rows = key_piece.shape[0]
    key_rows = key_piece[:, :inner_width].reshape(piece_rows, head_count, head_width)
    value_rows = key_piece[:, inner_width:].reshape(piece_rows, head_count, head_width)
    scores = (
        jnp.einsum("qhd,khd->hqk", queries, key_rows, preferred_element_type=jnp.float32) * 0.125
    )
    positions = piece_start + jnp.arange(piece_rows, dtype=jnp.int32)
    keep_mask = (positions < own_start) | (positions >= own_start + own_count)
    scores = jnp.where(keep_mask[None, None, :], scores, -2e30)
    highest = jnp.maximum(running_max, jnp.max(scores, axis=-1))
    shrink = jnp.exp(running_max - highest)
    chances = jnp.exp(scores - highest[:, :, None])
    total_mass = total_mass * shrink + jnp.sum(chances, axis=-1)
    update = jnp.einsum(
        "hqk,khd->qhd", chances.astype(jnp.bfloat16), value_rows, preferred_element_type=jnp.float32
    )
    weighted = weighted * jnp.transpose(shrink)[:, :, None] + update
    return (highest, total_mass, weighted)


def local(latents, stale_kv, stale_moments, norm_gain, norm_shift, w_qkv, w_out, out_bias):
    row_count, feature_width = latents.shape
    group_count = stale_moments.shape[1] // 2
    group_size = feature_width // group_count
    strips = lax.axis_size("patch")
    own_index = lax.axis_index("patch")
    grouped = latents.astype(jnp.float32).reshape(row_count, group_count, group_size)
    fresh_moments = jnp.concatenate(
        [jnp.sum(grouped, axis=(0, 2)), jnp.sum(grouped * grouped, axis=(0, 2))]
    )
    overall = lax.psum(stale_moments[0], "patch")
    totals = fresh_moments + (overall - stale_moments[0])
    element_count = float(strips * row_count * group_size)
    group_mean = totals[:group_count] / element_count
    spread = totals[group_count:] / element_count - group_mean * group_mean
    inverse_std = lax.rsqrt(spread + 1e-06)
    normed = ((grouped - group_mean[None, :, None]) * inverse_std[None, :, None]).reshape(
        row_count, feature_width
    )
    normed = (normed * norm_gain + norm_shift).astype(jnp.bfloat16)
    projected = jnp.dot(normed, w_qkv, preferred_element_type=jnp.float32).astype(jnp.bfloat16)
    inner_width = projected.shape[1] // 3
    head_count = inner_width // HDIM
    queries = projected[:, :inner_width].reshape(row_count, head_count, HDIM)
    fresh_kv = projected[:, inner_width:]
    initial = (
        jnp.full((head_count, row_count), -1e30, jnp.float32),
        jnp.zeros((head_count, row_count), jnp.float32),
        jnp.zeros((row_count, head_count, HDIM), jnp.float32),
    )
    local_state = absorb(initial, queries, fresh_kv, 0, 0, 0)
    own_start = own_index * row_count
    all_stale = lax.all_gather(stale_kv, "patch", axis=0, tiled=True)
    block_rows = math.gcd(all_stale.shape[0], 512)

    def one_block(block_index, state):
        block_start = block_index * block_rows
        key_piece = lax.dynamic_slice_in_dim(all_stale, block_start, block_rows, 0)
        return absorb(state, queries, key_piece, block_start, own_start, row_count)

    running_max, total_mass, weighted = lax.fori_loop(
        0, all_stale.shape[0] // block_rows, one_block, local_state
    )
    attended = (
        (weighted / jnp.transpose(total_mass)[:, :, None])
        .reshape(row_count, inner_width)
        .astype(jnp.bfloat16)
    )
    attention_out = (
        jnp.dot(attended, w_out, preferred_element_type=jnp.float32) + out_bias
    ).astype(jnp.bfloat16)
    return (attention_out, fresh_kv)


def solution(mesh):
    in_specs = (
        P(("groups", "patch"), None),
        P(("groups", "patch"), None),
        P(("groups", "patch"), None),
        P(),
        P(),
        P(),
        P(),
        P(),
    )
    out_specs = (P(("groups", "patch"), None), P(("groups", "patch"), None))
    return jax.shard_map(local, mesh=mesh, in_specs=in_specs, out_specs=out_specs, check_vma=False)
```

profile of v0, /device:TPU:0, one launch (start us, length us, event | category | flops | bytes accessed | tf_op | source)
XLA Modules:
  0.0 98.4 jit_solution(17484700348278659563)
XLA Ops:
  7.2 0.7 all-gather.2.cloned.1.call-update
  7.9 1.0 %convert_reduce_fusion = (f32[1280]{0:T(1024)S(1)}, f32[1280]{0:T(1024)S(1)}) fusion(bf16[88,1280]{1,0:T(8,128)(2,1)} %param.10), kind=kLoop, calls=%fused_computation.22 | loop fusion | flops 448000 | bytes 235520 | tf_op jit(solution)/shard_map/reduce_sum | solution.py:44
  9.3 35.4 %psum.7 = f32[64]{0:T(128)S(1)} all-reduce(f32[64]{0:T(128)} %bitcast.54), channel_id=1, replica_groups=mesh['groups'=2,'patch'=16] {'patch'}, use_global_device_ids=true, to_apply=%region_4.5 | all-reduce | flops 64 | bytes 512 | tf_op jit(solution)/shard_map/psum | solution.py:46
  44.7 0.7 maximum_add_fusion
  45.9 3.5 %convolution_convert_fusion = bf16[88,1920]{1,0:T(8,128)(2,1)S(1)} fusion(bf16[1280,1920]{1,0:T(8,128)(2,1)} %param.15, bf16[88,1280]{1,0:T(8,128)(2,1)} %param.10, f32[1280]{0:T(1024)} %param.14, f32[1280]{0:T(1024)} %param.13, f32[1280]{0:T(1024)S(1)} %mul.92, f32[1280]{0:T(1024)S(1)} %sub.64), kind=kOutput, calls=%fused_computation.16 | convolution fusion | flops 433382400 | bytes 5498880 | tf_op jit(solution)/shard_map/dot_general | solution.py:56
  49.4 0.7 slice.45
  51.4 9.1 %all-gather.2.cloned.1.call-done = bf16[1408,1280]{1,0:T(8,128)(2,1)} async-done(((bf16[88,1280]{1,0:T(8,128)(2,1)}), bf16[1408,1280]{1,0:T(8,128)(2,1)}) %all-gather.2.cloned.1.call-update) | async-done | bytes 3604496 | tf_op jit(solution)/shard_map/all_gather | solution.py:68
  60.5 29.9 %while.18 = (s32[]{:T(128)}, f32[10,88]{1,0:T(8,128)S(1)}, f32[10,88]{1,0:T(8,128)S(1)}, f32[88,10,64]{0,2,1:T(8,128)S(1)}, s32[]{:T(128)}, /*index=5*/s32[]{:T(...) while((s32[]{:T(128)}, f32[10,88]{1,0:T(8,128)S(1)}, ...), condition=%wide.region_10.11_spmd, body=%wide.region_7.10_spmd.sunk | while | flops 29740120 | bytes 3610059 | solution.py:76
  60.5 1.0 %fusion.52 = (bf16[128,640]{1,0:T(8,128)(2,1)S(1)}, bf16[128,640]{1,0:T(8,128)(2,1)S(1)}) fusion(bf16[1408,1280]{1,0:T(8,128)(2,1)} %get-tuple-element.312, s32[]{:T(128)S(6)} %select_n.26, s32[]{:T(128)S(6)} %add.146), kind=kLoop, calls=%fused_computation.44.clone.1 | loop fusion | bytes 655368 | tf_op jit(solution)/shard_map/while/body/eval_jaxpr/slice | solution.py:18
  61.9 0.5 fusion.53
  62.4 0.4 fusion.55
  62.8 0.4 fusion.56
  63.2 1.0 %fusion.52 = (bf16[128,640]{1,0:T(8,128)(2,1)S(1)}, bf16[128,640]{1,0:T(8,128)(2,1)S(1)}) fusion(bf16[1408,1280]{1,0:T(8,128)(2,1)} %get-tuple-element.312, s32[]{:T(128)S(6)} %select_n.26, s32[]{:T(128)S(6)} %add.146), kind=kLoop, calls=%fused_computation.44.clone.1 | loop fusion | bytes 655368 | tf_op jit(solution)/shard_map/while/body/eval_jaxpr/slice | solution.py:18
  64.6 0.5 fusion.53
  65.1 0.4 fusion.55
  65.5 0.4 fusion.56
  65.9 1.0 %fusion.52 = (bf16[128,640]{1,0:T(8,128)(2,1)S(1)}, bf16[128,640]{1,0:T(8,128)(2,1)S(1)}) fusion(bf16[1408,1280]{1,0:T(8,128)(2,1)} %get-tuple-element.312, s32[]{:T(128)S(6)} %select_n.26, s32[]{:T(128)S(6)} %add.146), kind=kLoop, calls=%fused_computation.44.clone.1 | loop fusion | bytes 655368 | tf_op jit(solution)/shard_map/while/body/eval_jaxpr/slice | solution.py:18
  67.3 0.5 fusion.53
  67.8 0.4 fusion.55
  68.2 0.4 fusion.56
  68.7 1.0 %fusion.52 = (bf16[128,640]{1,0:T(8,128)(2,1)S(1)}, bf16[128,640]{1,0:T(8,128)(2,1)S(1)}) fusion(bf16[1408,1280]{1,0:T(8,128)(2,1)} %get-tuple-element.312, s32[]{:T(128)S(6)} %select_n.26, s32[]{:T(128)S(6)} %add.146), kind=kLoop, calls=%fused_computation.44.clone.1 | loop fusion | bytes 655368 | tf_op jit(solution)/shard_map/while/body/eval_jaxpr/slice | solution.py:18
  70.0 0.5 fusion.53
  70.5 0.4 fusion.55
  70.9 0.4 fusion.56
  71.4 1.0 %fusion.52 = (bf16[128,640]{1,0:T(8,128)(2,1)S(1)}, bf16[128,640]{1,0:T(8,128)(2,1)S(1)}) fusion(bf16[1408,1280]{1,0:T(8,128)(2,1)} %get-tuple-element.312, s32[]{:T(128)S(6)} %select_n.26, s32[]{:T(128)S(6)} %add.146), kind=kLoop, calls=%fused_computation.44.clone.1 | loop fusion | bytes 655368 | tf_op jit(solution)/shard_map/while/body/eval_jaxpr/slice | solution.py:18
  72.8 0.5 fusion.53
  73.2 0.4 fusion.55
  73.7 0.4 fusion.56
  74.1 1.0 %fusion.52 = (bf16[128,640]{1,0:T(8,128)(2,1)S(1)}, bf16[128,640]{1,0:T(8,128)(2,1)S(1)}) fusion(bf16[1408,1280]{1,0:T(8,128)(2,1)} %get-tuple-element.312, s32[]{:T(128)S(6)} %select_n.26, s32[]{:T(128)S(6)} %add.146), kind=kLoop, calls=%fused_computation.44.clone.1 | loop fusion | bytes 655368 | tf_op jit(solution)/shard_map/while/body/eval_jaxpr/slice | solution.py:18
  75.5 0.5 fusion.53
  76.0 0.4 fusion.55
  76.4 0.4 fusion.56
  76.8 1.0 %fusion.52 = (bf16[128,640]{1,0:T(8,128)(2,1)S(1)}, bf16[128,640]{1,0:T(8,128)(2,1)S(1)}) fusion(bf16[1408,1280]{1,0:T(8,128)(2,1)} %get-tuple-element.312, s32[]{:T(128)S(6)} %select_n.26, s32[]{:T(128)S(6)} %add.146), kind=kLoop, calls=%fused_computation.44.clone.1 | loop fusion | bytes 655368 | tf_op jit(solution)/shard_map/while/body/eval_jaxpr/slice | solution.py:18
  78.2 0.5 fusion.53
  78.7 0.4 fusion.55
  79.5 1.0 %fusion.52 = (bf16[128,640]{1,0:T(8,128)(2,1)S(1)}, bf16[128,640]{1,0:T(8,128)(2,1)S(1)}) fusion(bf16[1408,1280]{1,0:T(8,128)(2,1)} %get-tuple-element.312, s32[]{:T(128)S(6)} %select_n.26, s32[]{:T(128)S(6)} %add.146), kind=kLoop, calls=%fused_computation.44.clone.1 | loop fusion | bytes 655368 | tf_op jit(solution)/shard_map/while/body/eval_jaxpr/slice | solution.py:18
  80.9 0.5 fusion.53
  81.4 0.4 fusion.55
  82.3 1.0 %fusion.52 = (bf16[128,640]{1,0:T(8,128)(2,1)S(1)}, bf16[128,640]{1,0:T(8,128)(2,1)S(1)}) fusion(bf16[1408,1280]{1,0:T(8,128)(2,1)} %get-tuple-element.312, s32[]{:T(128)S(6)} %select_n.26, s32[]{:T(128)S(6)} %add.146), kind=kLoop, calls=%fused_computation.44.clone.1 | loop fusion | bytes 655368 | tf_op jit(solution)/shard_map/while/body/eval_jaxpr/slice | solution.py:18
  83.6 0.5 fusion.53
  84.1 0.4 fusion.55
  85.0 1.0 %fusion.52 = (bf16[128,640]{1,0:T(8,128)(2,1)S(1)}, bf16[128,640]{1,0:T(8,128)(2,1)S(1)}) fusion(bf16[1408,1280]{1,0:T(8,128)(2,1)} %get-tuple-element.312, s32[]{:T(128)S(6)} %select_n.26, s32[]{:T(128)S(6)} %add.146), kind=kLoop, calls=%fused_computation.44.clone.1 | loop fusion | bytes 655368 | tf_op jit(solution)/shard_map/while/body/eval_jaxpr/slice | solution.py:18
  86.4 0.5 fusion.53
  86.8 0.4 fusion.55
  87.7 1.0 %fusion.52 = (bf16[128,640]{1,0:T(8,128)(2,1)S(1)}, bf16[128,640]{1,0:T(8,128)(2,1)S(1)}) fusion(bf16[1408,1280]{1,0:T(8,128)(2,1)} %get-tuple-element.312, s32[]{:T(128)S(6)} %select_n.26, s32[]{:T(128)S(6)} %add.146), kind=kLoop, calls=%fused_computation.44.clone.1 | loop fusion | bytes 655368 | tf_op jit(solution)/shard_map/while/body/eval_jaxpr/slice | solution.py:18
  89.1 0.5 fusion.53
  89.6 0.4 fusion.55
  90.5 1.1 %fusion.8 = bf16[88,1280]{1,0:T(8,128)(2,1)} fusion(bf16[88,640]{0,1:T(8,128)(2,1)S(1)} %bitcast.51, bf16[640,1280]{1,0:T(8,128)(2,1)S(1)} %copy-done, f32[1280]{0:T(1024)S(1)} %copy-done.1), kind=kOutput, calls=%fused_computation.15 | convolution fusion | flops 144404480 | bytes 1981440 | tf_op jit(solution)/shard_map/dot_general | solution.py:85
  (95 shorter events, 8.1 us)
Async XLA Ops:
  7.2 83.3 %copy-start = (bf16[640,1280]{1,0:T(8,128)(2,1)S(1)}, bf16[640,1280]{1,0:T(8,128)(2,1)}, u32[]{:S(2)}) copy-start(bf16[640,1280]{1,0:T(8,128)(2,1)} %param.16) | copy-start | bytes 4915204
  7.2 53.3 %all-gather.2.cloned.1.call-start = ((), (), s32[]{:S(2)}) async-start(), calls=%async_computation | async-start | bytes 3829760 | tf_op jit(solution)/shard_map/all_gather | solution.py:68
  60.5 30.0 %copy-start.1 = (f32[1280]{0:T(1024)S(1)}, f32[1280]{0:T(1024)}, u32[]{:S(2)}) copy-start(f32[1280]{0:T(1024)} %param.17) | copy-start | bytes 15364
Sparse Core Ops, SparseCore 0:
  10.2 50.2 all-gather.1
where the time goes:
time: 98.8 us; the launch traced here: 98.4 us
  blocking collectives  35.4 us (36%)
  local copies, waits for them, and re-layouts  16.9 us (17%)
  matrix products  14.3 us (14%)
  between operations  14.1 us (14%)
  waiting for transfers between devices  9.82 us (10%)
  other arithmetic  7.06 us (7%)
    psum x1, blocking collectives, local(): overall = lax.psum(stale_moments[0], 'patch')  35.4 us
    slice x13, local copies, waits for them, and re-layouts, absorb(): key_piece[:, inner_width:].reshape(piece_rows, head_count, head_width)  11.6 us
    all_gather x1, waiting for transfers between devices, local(): all_stale = lax.all_gather(stale_kv, 'patch', axis=0, tiled=True)  9.14 us
    dot_general x12, matrix products, absorb(): jnp.einsum('qhd,khd->hqk', queries, key_rows, preferred_element_type=jnp....  5.37 us
    reduce_sum x12, other arithmetic, absorb(): total_mass = total_mass * shrink + jnp.sum(chances, axis=-1)  4.63 us
    dot_general x12, matrix products, absorb(): jnp.einsum('hqk,khd->qhd', chances.astype(jnp.bfloat16), value_rows, pref...  4.33 us
    while x33, local copies, waits for them, and re-layouts  3.78 us
    dot_general x1, matrix products, local(): jnp.dot(normed, w_qkv, preferred_element_type=jnp.float32)  3.51 us
  transfers between devices with their start and end apart: 1, of which 1 were waited for; matrix products, arithmetic and copies ran while one was open for 8% of the time, Pallas kernels for 0%

commit v1 on v0

v1 whole, which is shorter than its diff:
```python
import functools

import jax
import jax.numpy as jnp
from jax import lax
from jax.experimental import pallas as pl
from jax.experimental.pallas import tpu as pltpu
from jax.sharding import PartitionSpec as P

MESH = pl.DeviceIdType.MESH
PAIR = 128
QUAD = 4
WAYS = 4
NEG = -1e30
F32 = jnp.float32
BF16 = jnp.bfloat16


def dot_t(a, b):
    return lax.dot_general(a, b, (((1,), (1,)), ((), ())), preferred_element_type=F32)


def thirds(row):
    high = row.astype(BF16).astype(F32)
    rest = row - high
    mid = rest.astype(BF16).astype(F32)
    return high, mid, rest - mid


def kernel(
    n, rows, pad,
    x_ref, stale_ref, mom_ref, gain_ref, shift_ref, wqkv_ref, wout_ref, bias_ref,
    out_ref, fresh_ref,
    sb, kv, momb, qs, qb, ob, og, wq, wo,
    mom_send, mom_recv, kv_send, kv_recv, core_send, side_send,
    q_send, q_recv, o_send, o_recv, w_sem,
):
    width = x_ref.shape[1]
    inner = stale_ref.shape[1] // 2
    me = lax.axis_index("patch")
    quad = lax.rem(me, QUAD)
    row = me // QUAD
    way = lax.rem(row, WAYS)
    block = row // WAYS
    lines = n // QUAD
    blocks = lines // WAYS

    weight_copies = [
        pltpu.make_async_copy(
            wqkv_ref.at[:, pl.ds(i * inner, inner)], wq.at[i], w_sem.at[i]
        )
        for i in range(3)
    ]
    out_copy = pltpu.make_async_copy(wout_ref, wo, w_sem.at[3])
    for copy in weight_copies:
        copy.start()
    out_copy.start()

    barrier = pltpu.get_barrier_semaphore()

    def greet(i, carry):
        pl.semaphore_signal(
            barrier, inc=1, device_id={"patch": lax.rem(me + 1 + i, n)}, device_id_type=MESH
        )
        return carry

    lax.fori_loop(0, n - 1, greet, 0, unroll=True)

    momb[me] = jnp.broadcast_to(mom_ref[...], (8, mom_ref.shape[1]))
    tail = jnp.zeros((pad - rows, PAIR), F32)

    def piece(c):
        part = stale_ref[:, c * PAIR:(c + 1) * PAIR].astype(F32)
        return jnp.concatenate([part, tail], axis=0).astype(BF16)

    pairs = inner // PAIR
    for w in range(WAYS):
        sb[w, 0] = piece(w)
        sb[w, 1] = piece(pairs + w)
        sb[w, 2] = piece(WAYS)
        sb[w, 3] = piece(pairs + WAYS)
    kv[me] = sb[way]

    pl.semaphore_wait(barrier, n - 1)

    def mom_copy(i):
        peer = lax.rem(me + 1 + i, n)
        return pltpu.make_async_remote_copy(
            src_ref=momb.at[me], dst_ref=momb.at[me],
            send_sem=mom_send.at[i], recv_sem=mom_recv.at[me],
            device_id={"patch": peer}, device_id_type=MESH,
        )

    def mom_wait(i):
        peer = lax.rem(me + 1 + i, n)
        return pltpu.make_async_remote_copy(
            src_ref=momb.at[peer], dst_ref=momb.at[peer],
            send_sem=mom_send.at[i], recv_sem=mom_recv.at[peer],
            device_id={"patch": peer}, device_id_type=MESH,
        )

    def line_row(k):
        return lax.rem(row + k, lines)

    def line_copy(k):
        peer_row = line_row(k)
        return pltpu.make_async_remote_copy(
            src_ref=sb.at[lax.rem(peer_row, WAYS)], dst_ref=kv.at[me],
            send_sem=kv_send.at[k], recv_sem=kv_recv.at[me],
            device_id={"patch": peer_row * QUAD + quad}, device_id_type=MESH,
        )

    core_quad = quad + 1 - 2 * lax.rem(quad, 2)
    side_quad = lax.rem(quad + 2, QUAD)
    far_quad = lax.rem(core_quad + 2, QUAD)

    def slot_copy(slot, sems, to_quad):
        return pltpu.make_async_remote_copy(
            src_ref=kv.at[slot], dst_ref=kv.at[slot],
            send_sem=sems.at[slot], recv_sem=kv_recv.at[slot],
            device_id={"patch": row * QUAD + to_quad}, device_id_type=MESH,
        )

    def pair_copy(k, src, dst, send, recv):
        peer_way = lax.rem(way + k, WAYS)
        return pltpu.make_async_remote_copy(
            src_ref=src.at[peer_way], dst_ref=dst.at[way],
            send_sem=send.at[k], recv_sem=recv.at[way],
            device_id={"patch": (block * WAYS + peer_way) * QUAD + quad},
            device_id_type=MESH,
        )

    def pair_wait(k, src, dst, send, recv):
        peer_way = lax.rem(way + k, WAYS)
        return pltpu.make_async_remote_copy(
            src_ref=dst.at[peer_way], dst_ref=dst.at[peer_way],
            send_sem=send.at[k], recv_sem=recv.at[peer_way],
            device_id={"patch": (block * WAYS + peer_way) * QUAD + quad},
            device_id_type=MESH,
        )

    for i in range(n - 1):
        mom_copy(i).start()
    for k in range(1, lines):
        line_copy(k).start()
    slot_copy(me, side_send, side_quad).start()
    slot_copy(me, core_send, core_quad).start()

    count = mom_ref.shape[1]
    groups = count // 2
    size = width // groups
    x = x_ref[...].astype(F32)
    first = jnp.sum(x, axis=0, keepdims=True)
    second = jnp.sum(x * x, axis=0, keepdims=True)
    lane = lax.broadcasted_iota(jnp.int32, (PAIR, width), 1)
    low = lax.rem(lax.broadcasted_iota(jnp.int32, (PAIR, width), 0), groups) * size
    member = jnp.where((lane >= low) & (lane < low + size), 1.0, 0.0).astype(BF16)
    zero = jnp.zeros((1, width), F32)
    table = jnp.concatenate([*thirds(first), *thirds(second), zero, zero], axis=0)
    sums = dot_t(table.astype(BF16), member)
    head = lax.broadcasted_iota(jnp.int32, (1, PAIR), 1)
    fresh_moments = jnp.where(
        head < groups, sums[0:1] + sums[1:2] + sums[2:3], sums[3:4] + sums[4:5] + sums[5:6]
    )
    stale_sum = jnp.zeros((8, count), F32)
    for i in range(n - 1):
        mom_wait(i).wait_recv()
        stale_sum = stale_sum + momb[lax.rem(me + 1 + i, n)]
    stale_row = jnp.concatenate(
        [stale_sum[0:1], jnp.zeros((1, PAIR - count), F32)], axis=1
    )
    totals = fresh_moments + stale_row
    left = jnp.where(head < groups, totals, 0.0)
    right = jnp.where((head >= groups) & (head < count), totals, 0.0)
    none = jnp.zeros((1, PAIR), F32)
    table = jnp.concatenate([*thirds(left), *thirds(right), none, none], axis=0)
    spreadout = jnp.dot(table.astype(BF16), member, preferred_element_type=F32)
    element_count = float(n * rows * size)
    mean = (spreadout[0:1] + spreadout[1:2] + spreadout[2:3]) / element_count
    spread = (spreadout[3:4] + spreadout[4:5] + spreadout[5:6]) / element_count - mean * mean
    inverse = lax.rsqrt(spread + 1e-06)
    normed = ((x - mean) * inverse) * gain_ref[...] + shift_ref[...]
    normed = jnp.concatenate([normed, jnp.zeros((pad - rows, width), F32)], axis=0).astype(BF16)

    weight_copies[0].wait()
    queries = jnp.dot(normed, wq[0], preferred_element_type=F32).astype(BF16)
    queries = (queries.astype(F32) * 0.125).astype(BF16)
    for w in range(WAYS):
        qs[w] = queries[:, w * PAIR:(w + 1) * PAIR]
    qb[way] = qs[way]
    for k in range(1, WAYS):
        pair_copy(k, qs, qb, q_send, q_recv).start()

    def forward(k):
        slot = line_row(k) * QUAD + quad
        slot_copy(slot, side_send, side_quad).wait_recv()
        slot_copy(slot, side_send, side_quad).start()
        slot_copy(slot, core_send, core_quad).start()

    order = [1, lines - 1] + list(range(2, lines - 1))
    forward(order[0])
    weight_copies[1].wait()
    keys = jnp.dot(normed, wq[1], preferred_element_type=F32).astype(BF16)
    fresh_ref[:, :inner] = keys[:rows]
    forward(order[1])
    weight_copies[2].wait()
    values = jnp.dot(normed, wq[2], preferred_element_type=F32).astype(BF16)
    fresh_ref[:, inner:] = values[:rows]
    for k in order[2:]:
        forward(k)

    half = lax.broadcasted_iota(jnp.int32, (1, PAIR), 1) < PAIR // 2

    def one_head(query, key, value, biases):
        scores = dot_t(query, key)
        if len(biases) == 1:
            scores = scores + biases[0]
        else:
            scores = jnp.concatenate(
                [scores[i * pad:(i + 1) * pad] + b for i, b in enumerate(biases)], axis=0
            )
        top = jnp.max(scores, axis=1, keepdims=True)
        chances = jnp.exp(scores - top)
        mass = jnp.sum(chances, axis=1, keepdims=True)
        weighted = jnp.dot(chances.astype(BF16), value, preferred_element_type=F32)
        return top + jnp.log(mass), weighted / mass

    def attend(query, key, value, biases):
        none = jnp.zeros_like(query)
        lse0, out0 = one_head(jnp.where(half, query, none), key, value, biases)
        lse1, out1 = one_head(jnp.where(half, none, query), key, value, biases)
        return jnp.where(half, lse0, lse1), jnp.where(half, out0, out1)

    def merge(a, b):
        top = jnp.maximum(a[0], b[0])
        wa = jnp.exp(a[0] - top)
        wb = jnp.exp(b[0] - top)
        mass = wa + wb
        return top + jnp.log(mass), (wa * a[1] + wb * b[1]) / mass

    key_lane = lax.broadcasted_iota(jnp.int32, (1, pad), 1)
    own_bias = jnp.where(key_lane < rows, 0.0, NEG)
    fresh = []
    for p in range(pairs):
        cut = slice(p * PAIR, (p + 1) * PAIR)
        fresh.append(attend(queries[:, cut], keys[:, cut], values[:, cut], [own_bias]))

    for k in range(lines):
        slot = line_row(k) * QUAD + side_quad
        slot_copy(slot, side_send, side_quad).wait_recv()
        slot_copy(slot, core_send, core_quad).start()
    for k in range(lines):
        slot_copy(line_row(k) * QUAD + core_quad, core_send, core_quad).wait_recv()
    for k in range(lines):
        slot_copy(line_row(k) * QUAD + far_quad, core_send, core_quad).wait_recv()
    for k in range(1, WAYS):
        pair_wait(k, qs, qb, q_send, q_recv).wait_recv()

    step = n // blocks
    span = step * pad
    position = lax.broadcasted_iota(jnp.int32, (1, span), 1)
    padding = jnp.where(lax.rem(position, pad) < rows, 0.0, NEG)

    def bias_for(owner, b):
        start = (owner - b * step) * pad
        return jnp.where((position >= start) & (position < start + pad), NEG, padding)

    def stale_part(query, part, owners):
        def one(b):
            key = kv[pl.ds(b * step, step), part].reshape(span, PAIR)
            value = kv[pl.ds(b * step, step), part + 1].reshape(span, PAIR)
            return attend(query, key, value, [bias_for(o, b) for o in owners])

        state = one(0)
        if blocks > 1:
            state = lax.fori_loop(1, blocks, lambda b, s: merge(s, one(b)), state)
        return state

    owners = [(block * WAYS + w) * QUAD + quad for w in range(WAYS)]
    all_queries = qb[...].reshape(WAYS * pad, PAIR)
    lse, part = stale_part(all_queries, 0, owners)
    for w in range(WAYS):
        cut = slice(w * pad, (w + 1) * pad)
        flat = jnp.transpose(
            jnp.concatenate([lse[cut], jnp.zeros((PAIR - pad, PAIR), F32)], axis=0)
        )
        none = jnp.zeros((1, PAIR), F32)
        stats = jnp.concatenate(
            [*thirds(flat[0:1]), *thirds(flat[PAIR // 2:PAIR // 2 + 1]), none, none], axis=0
        )
        og[w] = jnp.concatenate([part[cut][:rows], stats], axis=0).astype(BF16)
    for k in range(1, WAYS):
        pair_copy(k, og, ob, o_send, o_recv).start()
    ob[way] = og[way]

    last = merge(fresh[WAYS], stale_part(queries[:, WAYS * PAIR:], 2, [me]))[1]

    for k in range(1, WAYS):
        pair_wait(k, og, ob, o_send, o_recv).wait_recv()
    heads = []
    for p in range(WAYS):
        got = ob[p].astype(F32)
        stats = got[rows:pad]
        lse0 = stats[0:1] + stats[1:2] + stats[2:3]
        lse1 = stats[3:4] + stats[4:5] + stats[5:6]
        flat = jnp.transpose(
            jnp.concatenate(
                [jnp.broadcast_to(lse0, (PAIR // 2, PAIR)), jnp.broadcast_to(lse1, (PAIR // 2, PAIR))],
                axis=0,
            )
        )[:pad]
        heads.append(merge(fresh[p], (flat, got))[1].astype(BF16))
    heads.append(last.astype(BF16))
    attended = jnp.concatenate(heads, axis=1)
    out_copy.wait()
    result = jnp.dot(attended, wo[...], preferred_element_type=F32) + bias_ref[...]
    out_ref[...] = result.astype(BF16)[:rows]

    for i in range(n - 1):
        mom_copy(i).wait_send()
    for k in range(1, lines):
        line_copy(k).wait_send()
    for k in range(lines):
        slot = line_row(k) * QUAD + quad
        slot_copy(slot, side_send, side_quad).wait_send()
        slot_copy(slot, core_send, core_quad).wait_send()
        slot = line_row(k) * QUAD + side_quad
        slot_copy(slot, core_send, core_quad).wait_send()
    for k in range(1, WAYS):
        pair_copy(k, qs, qb, q_send, q_recv).wait_send()
        pair_copy(k, og, ob, o_send, o_recv).wait_send()


def solution(mesh):
    n = mesh.shape["patch"]

    def local(latents, stale_kv, stale_moments, norm_gain, norm_shift, w_qkv, w_out, out_bias):
        rows, width = latents.shape
        inner = w_out.shape[0]
        pad = -(-rows // 16) * 16
        vmem = pl.BlockSpec(memory_space=pltpu.VMEM)
        hbm = pl.BlockSpec(memory_space=pl.ANY)
        dma = pltpu.SemaphoreType.DMA
        return pl.pallas_call(
            functools.partial(kernel, n, rows, pad),
            out_shape=(
                jax.ShapeDtypeStruct((rows, w_out.shape[1]), BF16),
                jax.ShapeDtypeStruct((rows, 2 * inner), BF16),
            ),
            in_specs=[vmem, vmem, vmem, vmem, vmem, hbm, hbm, vmem],
            out_specs=(vmem, vmem),
            scratch_shapes=[
                pltpu.VMEM((WAYS, 4, pad, PAIR), BF16),
                pltpu.VMEM((n, 4, pad, PAIR), BF16),
                pltpu.VMEM((n, 8, stale_moments.shape[1]), F32),
                pltpu.VMEM((WAYS, pad, PAIR), BF16),
                pltpu.VMEM((WAYS, pad, PAIR), BF16),
                pltpu.VMEM((WAYS, pad, PAIR), BF16),
                pltpu.VMEM((WAYS, pad, PAIR), BF16),
                pltpu.VMEM((3, width, inner), BF16),
                pltpu.VMEM(w_out.shape, BF16),
                dma((n,)), dma((n,)), dma((n // QUAD,)), dma((n,)), dma((n,)), dma((n,)),
                dma((WAYS,)), dma((WAYS,)), dma((WAYS,)), dma((WAYS,)), dma((4,)),
            ],
            compiler_params=pltpu.CompilerParams(
                collective_id=0, has_side_effects=True, vmem_limit_bytes=52 * 1024 * 1024
            ),
        )(
            latents, stale_kv, stale_moments, norm_gain[None], norm_shift[None],
            w_qkv, w_out, out_bias[None],
        )

    strip = P(("groups", "patch"), None)
    return jax.shard_map(
        local,
        mesh=mesh,
        in_specs=(strip, strip, strip, P(), P(), P(), P(), P()),
        out_specs=(strip, strip),
        check_vma=False,
    )
```

time: 98.8 us -> 39.6 us (0.40)
  blocking collectives: 35.4 us -> 0 us
  Pallas kernels: 0 us -> 32.5 us
  matrix products: 14.3 us -> 0 us
  between operations: 14.1 us -> 0.64 us
  local copies, waits for them, and re-layouts: 16.9 us -> 6.01 us
  waiting for transfers between devices: 9.82 us -> 0 us
  other arithmetic: 7.06 us -> 0 us
    psum x1 -> x0, blocking collectives: 35.4 us -> none  [local(): overall = lax.psum(stale_moments[0], 'patch')]
    pallas_call x0 -> x1, Pallas kernels: none -> 32.5 us  [local(): pl.pallas_call(functools.partial(kernel, n, rows, pad), out_shape=(jax.Sh...]
    dot_general x26 -> x0, matrix products: 14.3 us -> none  [the longest x12 5.37 us: absorb(): jnp.einsum('qhd,khd->hqk', queries, key_rows, preferred_element_type=jnp....]
    slice x16 -> x0, local copies, waits for them, and re-layouts: 12.6 us -> none  [the longest x13 11.6 us: absorb(): key_piece[:, inner_width:].reshape(piece_rows, head_count, head_width)]
    all_gather x1 -> x0, waiting for transfers between devices: 9.14 us -> none  [local(): all_stale = lax.all_gather(stale_kv, 'patch', axis=0, tiled=True)]
    reduce_sum x15 -> x0, other arithmetic: 5.87 us -> none  [the longest x12 4.63 us: absorb(): total_mass = total_mass * shrink + jnp.sum(chances, axis=-1)]
    unnamed x4 -> x8, local copies, waits for them, and re-layouts: 0.01 us -> 3.9 us
    while x33 -> x0, local copies, waits for them, and re-layouts: 3.78 us -> none
  transfers between devices with their start and end apart: 1 -> 0, of which waited for: 1 -> 0; matrix products, arithmetic and copies ran while one was open for 8% -> 0% of each run, Pallas kernels for 0% -> 0%
where the time goes in v1:
time: 39.6 us; the launch traced here: 39.2 us
  Pallas kernels  32.5 us (82%)
  local copies, waits for them, and re-layouts  6.01 us (15%)
  between operations  0.64 us (2%)
    pallas_call x1, Pallas kernels, local(): pl.pallas_call(functools.partial(kernel, n, rows, pad), out_shape=(jax.Sh...  32.5 us
    unnamed x8, local copies, waits for them, and re-layouts  3.9 us

profile of v1, /device:TPU:0, one launch (start us, length us, event | category | flops | bytes accessed | tf_op | source)
XLA Modules:
  0.0 39.2 jit_solution(12603364828663143695)
XLA Ops:
  0.6 0.7 %broadcast_in_dim.9.gain_ref = f32[1,1280]{1,0:T(1,128)S(1)} reshape(f32[1280]{0:T(1024)} %param.11) | data formatting | bytes 10240 | tf_op jit(solution)/shard_map/broadcast_in_dim | solution.py:369
  1.3 0.7 %broadcast_in_dim.10.shift_ref = f32[1,1280]{1,0:T(1,128)S(1)} reshape(f32[1280]{0:T(1024)} %param.12) | data formatting | bytes 10240 | tf_op jit(solution)/shard_map/broadcast_in_dim | solution.py:369
  2.0 0.7 %broadcast_in_dim.11.bias_ref = f32[1,1280]{1,0:T(1,128)S(1)} reshape(f32[1280]{0:T(1024)} %param.15) | data formatting | bytes 10240 | tf_op jit(solution)/shard_map/broadcast_in_dim | solution.py:370
  2.7 0.0 copy-start
  2.7 0.9 %copy-done = bf16[88,1280]{1,0:T(8,128)(2,1)S(1)} copy-done((bf16[88,1280]{1,0:T(8,128)(2,1)S(1)}, bf16[88,1280]{1,0:T(8,128)(2,1)}, u32[]{:S(2)}) %copy-start) | copy-done | bytes 225304
  3.7 0.0 copy-start.1
  3.7 0.9 %copy-done.1 = bf16[88,1280]{1,0:T(8,128)(2,1)S(1)} copy-done((bf16[88,1280]{1,0:T(8,128)(2,1)S(1)}, bf16[88,1280]{1,0:T(8,128)(2,1)}, u32[]{:S(2)}) %copy-start.1) | copy-done | bytes 225304
  4.6 0.0 copy-start.2
  4.6 0.7 %copy-done.2 = f32[1,64]{1,0:T(1,128)S(1)} copy-done((f32[1,64]{1,0:T(1,128)S(1)}, f32[1,64]{1,0:T(1,128)}, u32[]{:S(2)}) %copy-start.2) | copy-done | bytes 280
  5.3 32.5 %shard_map.95 = (bf16[88,1280]{1,0:T(8,128)(2,1)S(1)}, bf16[88,1280]{1,0:T(8,128)(2,1)S(1)}) custom-call(bf16[88,1280]{1,0:T(8,128)(2,1)S(1)} %copy-done, bf16[88,1280]{1,0:T(8,128)(2,1)S(1)} %copy-done.1, f32[1,64]{1,0:T(1,128)S(1)} %copy-done.2, f32[1,1280]{1,0:T(1,128)S(1)} %broadcast_in_dim.9.gain_ref, f32[1,1280]{1,0:T(1,128)S(1)} %broadcast_in_dim.10.shift_ref, ...), custom_call_target="tpu_custom_call" | custom-call | tf_op jit(solution)/shard_map/pallas_call | solution.py:344
  37.8 0.7 %copy.12 = bf16[88,1280]{1,0:T(8,128)(2,1)} copy(bf16[88,1280]{1,0:T(8,128)(2,1)S(1)} %get-tuple-element.4) | data formatting | bytes 450560
  38.5 0.7 %copy.13 = bf16[88,1280]{1,0:T(8,128)(2,1)} copy(bf16[88,1280]{1,0:T(8,128)(2,1)S(1)} %get-tuple-element.5) | data formatting | bytes 450560
Async XLA Ops:
  2.7 0.9 %copy-start = (bf16[88,1280]{1,0:T(8,128)(2,1)S(1)}, bf16[88,1280]{1,0:T(8,128)(2,1)}, u32[]{:S(2)}) copy-start(bf16[88,1280]{1,0:T(8,128)(2,1)} %x_ref.1) | copy-start | bytes 675844
  3.7 0.9 %copy-start.1 = (bf16[88,1280]{1,0:T(8,128)(2,1)S(1)}, bf16[88,1280]{1,0:T(8,128)(2,1)}, u32[]{:S(2)}) copy-start(bf16[88,1280]{1,0:T(8,128)(2,1)} %stale_ref.1) | copy-start | bytes 675844
  4.6 0.7 %copy-start.2 = (f32[1,64]{1,0:T(1,128)S(1)}, f32[1,64]{1,0:T(1,128)}, u32[]{:S(2)}) copy-start(f32[1,64]{1,0:T(1,128)} %mom_ref.1) | copy-start | bytes 772

commit v2 on v1

v2 whole, which is shorter than its diff:
```python
import functools

import jax
import jax.numpy as jnp
from jax import lax
from jax.experimental import pallas as pl
from jax.experimental.pallas import tpu as pltpu
from jax.sharding import PartitionSpec as P

MESH = pl.DeviceIdType.MESH
PAIR = 128
CORES = 2
WAYS = 8
HOSTS = (2, 5)
NEG = -1e30
F32 = jnp.float32
BF16 = jnp.bfloat16


def dot_t(a, b):
    return lax.dot_general(a, b, (((1,), (1,)), ((), ())), preferred_element_type=F32)


def thirds(row):
    high = row.astype(BF16).astype(F32)
    rest = row - high
    mid = rest.astype(BF16).astype(F32)
    return high, mid, rest - mid


def kernel(
    n, rows, pad,
    x_hbm, stale_hbm, mom_hbm, gain_hbm, shift_hbm, wqkv_ref, wout_ref, bias_hbm,
    out_ref, fresh_ref,
    x_ref, stale_ref, mom_ref, gain_ref, shift_ref, bias_ref,
    sb, kv, kx, momb, qs, qb, qx, ob, og, ox, wq, wo,
    mom_send, mom_recv, kv_send, kv_recv, kx_send, kx_recv, core_send, corex_send,
    q_send, q_recv, qx_send, qx_recv, o_send, o_recv, ox_send, w_sem, in_sem,
):
    width = x_ref.shape[1]
    inner = stale_ref.shape[1] // 2
    me = lax.axis_index("patch")
    core = lax.rem(me, CORES)
    chip = me // CORES
    way = lax.rem(chip, WAYS)
    block = chip // WAYS
    lines = n // CORES
    blocks = lines // WAYS
    fold = pad // 2
    half = lax.broadcasted_iota(jnp.int32, (1, PAIR), 1) < PAIR // 2
    is_host = (way == HOSTS[0]) | (way == HOSTS[1])
    extra = jnp.where(way == HOSTS[1], WAYS + 1, WAYS)

    def swap(a):
        return pltpu.roll(a, PAIR // 2, 1)

    ins = [
        pltpu.make_async_copy(src, dst, in_sem.at[i])
        for i, (src, dst) in enumerate([
            (stale_hbm, stale_ref), (mom_hbm, mom_ref), (x_hbm, x_ref),
            (gain_hbm, gain_ref), (shift_hbm, shift_ref), (bias_hbm, bias_ref),
        ])
    ]
    for copy in ins:
        copy.start()
    weight_copies = [
        pltpu.make_async_copy(
            wqkv_ref.at[:, pl.ds(i * inner, inner)], wq.at[i], w_sem.at[i]
        )
        for i in range(3)
    ]
    out_copy = pltpu.make_async_copy(wout_ref, wo, w_sem.at[3])
    for copy in weight_copies:
        copy.start()
    out_copy.start()

    barrier = pltpu.get_barrier_semaphore()

    def greet(i, carry):
        pl.semaphore_signal(
            barrier, inc=1, device_id={"patch": lax.rem(me + 1 + i, n)}, device_id_type=MESH
        )
        return carry

    lax.fori_loop(0, n - 1, greet, 0, unroll=True)

    ins[0].wait()
    ins[1].wait()

    momb[me] = jnp.broadcast_to(mom_ref[...], (8, mom_ref.shape[1]))
    tail = jnp.zeros((pad - rows, PAIR), F32)

    def piece(c):
        part = stale_ref[:, c * PAIR:(c + 1) * PAIR].astype(F32)
        return jnp.concatenate([part, tail], axis=0)

    pairs = inner // PAIR
    for p in range(pairs):
        key, value = piece(p), piece(pairs + p)
        sb[2 * p] = jnp.where(half, key, swap(value)).astype(BF16)
        sb[2 * p + 1] = jnp.where(half, swap(key), value).astype(BF16)
    kv[me] = sb[way]

    @pl.when(is_host)
    def _():
        kx[me] = sb[extra]

    pl.semaphore_wait(barrier, n - 1)

    def mom_copy(i):
        peer = lax.rem(me + 1 + i, n)
        return pltpu.make_async_remote_copy(
            src_ref=momb.at[me], dst_ref=momb.at[me],
            send_sem=mom_send.at[i], recv_sem=mom_recv.at[me],
            device_id={"patch": peer}, device_id_type=MESH,
        )

    def mom_wait(i):
        peer = lax.rem(me + 1 + i, n)
        return pltpu.make_async_remote_copy(
            src_ref=momb.at[peer], dst_ref=momb.at[peer],
            send_sem=mom_send.at[i], recv_sem=mom_recv.at[peer],
            device_id={"patch": peer}, device_id_type=MESH,
        )

    def chip_at(k):
        return lax.rem(chip + k, lines)

    def line_copy(k):
        peer = chip_at(k)
        return pltpu.make_async_remote_copy(
            src_ref=sb.at[lax.rem(peer, WAYS)], dst_ref=kv.at[me],
            send_sem=kv_send.at[k], recv_sem=kv_recv.at[me],
            device_id={"patch": peer * CORES + core}, device_id_type=MESH,
        )

    def host_copy(e, b):
        peer = b * WAYS + HOSTS[e]
        return pltpu.make_async_remote_copy(
            src_ref=sb.at[WAYS + e], dst_ref=kx.at[me],
            send_sem=kx_send.at[e * blocks + b], recv_sem=kx_recv.at[me],
            device_id={"patch": peer * CORES + core}, device_id_type=MESH,
        )

    def core_copy(buf, slot, send, recv):
        return pltpu.make_async_remote_copy(
            src_ref=buf.at[slot], dst_ref=buf.at[slot],
            send_sem=send.at[slot], recv_sem=recv.at[slot],
            device_id={"patch": chip * CORES + 1 - core}, device_id_type=MESH,
        )

    def block_peer(w):
        return {"patch": (block * WAYS + w) * CORES + core}

    def way_copy(k, src, dst, send, recv):
        peer = lax.rem(way + k, WAYS)
        return pltpu.make_async_remote_copy(
            src_ref=src.at[peer], dst_ref=dst.at[way],
            send_sem=send.at[k], recv_sem=recv.at[way],
            device_id=block_peer(peer), device_id_type=MESH,
        )

    def way_wait(k, dst, send, recv):
        peer = lax.rem(way + k, WAYS)
        return pltpu.make_async_remote_copy(
            src_ref=dst.at[peer], dst_ref=dst.at[peer],
            send_sem=send.at[k], recv_sem=recv.at[peer],
            device_id=block_peer(peer), device_id_type=MESH,
        )

    def host_query(e):
        return pltpu.make_async_remote_copy(
            src_ref=qs.at[WAYS + e], dst_ref=qx.at[way],
            send_sem=qx_send.at[e], recv_sem=qx_recv.at[way],
            device_id=block_peer(HOSTS[e]), device_id_type=MESH,
        )

    def host_result(k):
        peer = lax.rem(way + k, WAYS)
        return pltpu.make_async_remote_copy(
            src_ref=ox.at[peer], dst_ref=ob.at[extra],
            send_sem=ox_send.at[k], recv_sem=o_recv.at[extra],
            device_id=block_peer(peer), device_id_type=MESH,
        )

    def host_result_wait(e):
        return pltpu.make_async_remote_copy(
            src_ref=ob.at[WAYS + e], dst_ref=ob.at[WAYS + e],
            send_sem=ox_send.at[0], recv_sem=o_recv.at[WAYS + e],
            device_id=block_peer(HOSTS[e]), device_id_type=MESH,
        )

    for i in range(n - 1):
        mom_copy(i).start()
    for e in range(2):
        for b in range(blocks):
            @pl.when(chip != b * WAYS + HOSTS[e])
            def _():
                host_copy(e, b).start()
    for k in range(1, lines):
        line_copy(k).start()
    core_copy(kv, me, core_send, kv_recv).start()

    @pl.when(is_host)
    def _():
        core_copy(kx, me, corex_send, kx_recv).start()

    count = mom_ref.shape[1]
    groups = count // 2
    size = width // groups
    for copy in ins[2:]:
        copy.wait()
    x = x_ref[...].astype(F32)
    first = jnp.sum(x, axis=0, keepdims=True)
    second = jnp.sum(x * x, axis=0, keepdims=True)
    lane = lax.broadcasted_iota(jnp.int32, (PAIR, width), 1)
    low = lax.rem(lax.broadcasted_iota(jnp.int32, (PAIR, width), 0), groups) * size
    member = jnp.where((lane >= low) & (lane < low + size), 1.0, 0.0).astype(BF16)
    zero = jnp.zeros((1, width), F32)
    table = jnp.concatenate([*thirds(first), *thirds(second), zero, zero], axis=0)
    sums = dot_t(table.astype(BF16), member)
    head = lax.broadcasted_iota(jnp.int32, (1, PAIR), 1)
    fresh_moments = jnp.where(
        head < groups, sums[0:1] + sums[1:2] + sums[2:3], sums[3:4] + sums[4:5] + sums[5:6]
    )
    stale_sum = jnp.zeros((8, count), F32)
    for i in range(n - 1):
        mom_wait(i).wait_recv()
        stale_sum = stale_sum + momb[lax.rem(me + 1 + i, n)]
    stale_row = jnp.concatenate(
        [stale_sum[0:1], jnp.zeros((1, PAIR - count), F32)], axis=1
    )
    totals = fresh_moments + stale_row
    left = jnp.where(head < groups, totals, 0.0)
    right = jnp.where((head >= groups) & (head < count), totals, 0.0)
    none = jnp.zeros((1, PAIR), F32)
    table = jnp.concatenate([*thirds(left), *thirds(right), none, none], axis=0)
    spreadout = jnp.dot(table.astype(BF16), member, preferred_element_type=F32)
    element_count = float(n * rows * size)
    mean = (spreadout[0:1] + spreadout[1:2] + spreadout[2:3]) / element_count
    spread = (spreadout[3:4] + spreadout[4:5] + spreadout[5:6]) / element_count - mean * mean
    inverse = lax.rsqrt(spread + 1e-06)
    normed = ((x - mean) * inverse) * gain_ref[...][None] + shift_ref[...][None]
    normed = jnp.concatenate([normed, jnp.zeros((pad - rows, width), F32)], axis=0).astype(BF16)

    weight_copies[0].wait()
    queries = jnp.dot(normed, wq[0], preferred_element_type=F32).astype(BF16)
    queries = (queries.astype(F32) * 0.125).astype(BF16)
    def folded(a):
        return jnp.where(half, a[:fold], swap(a[fold:]))

    for p in range(pairs):
        query = queries[:, p * PAIR:(p + 1) * PAIR].astype(F32)
        qs[2 * p] = folded(query).astype(BF16)
        qs[2 * p + 1] = folded(swap(query)).astype(BF16)
    qb[way] = qs[way]
    for k in range(1, WAYS):
        way_copy(k, qs, qb, q_send, q_recv).start()
    for e in range(2):
        @pl.when(way == HOSTS[e])
        def _():
            qx[way] = qs[WAYS + e]

        @pl.when(way != HOSTS[e])
        def _():
            host_query(e).start()

    weight_copies[1].wait()
    keys = jnp.dot(normed, wq[1], preferred_element_type=F32).astype(BF16)
    fresh_ref[:, :inner] = keys[:rows]
    weight_copies[2].wait()
    values = jnp.dot(normed, wq[2], preferred_element_type=F32).astype(BF16)
    fresh_ref[:, inner:] = values[:rows]

    def one_head(query, key, value, biases, seg):
        scores = dot_t(query, key)
        if len(biases) == 1:
            scores = scores + biases[0]
        else:
            scores = jnp.concatenate(
                [scores[i * seg:(i + 1) * seg] + b for i, b in enumerate(biases)], axis=0
            )
        top = jnp.max(scores, axis=1, keepdims=True)
        chances = jnp.exp(scores - top)
        mass = jnp.sum(chances, axis=1, keepdims=True)
        weighted = jnp.dot(chances.astype(BF16), value, preferred_element_type=F32)
        return top + jnp.log(mass), weighted / mass

    def attend(query, key, value, biases):
        none = jnp.zeros_like(query)
        lse0, out0 = one_head(jnp.where(half, query, none), key, value, biases, pad)
        lse1, out1 = one_head(jnp.where(half, none, query), key, value, biases, pad)
        return jnp.where(half, lse0, lse1), jnp.where(half, out0, out1)

    def merge(a, b):
        top = jnp.maximum(a[0], b[0])
        wa = jnp.exp(a[0] - top)
        wb = jnp.exp(b[0] - top)
        mass = wa + wb
        return top + jnp.log(mass), (wa * a[1] + wb * b[1]) / mass

    key_lane = lax.broadcasted_iota(jnp.int32, (1, pad), 1)
    own_bias = jnp.where(key_lane < rows, 0.0, NEG)
    fresh = []
    for p in range(pairs):
        cut = slice(p * PAIR, (p + 1) * PAIR)
        fresh.append(attend(queries[:, cut], keys[:, cut], values[:, cut], [own_bias]))

    def pass_on(buf, send, recv):
        for k in range(1, lines):
            copy = core_copy(buf, chip_at(k) * CORES + core, send, recv)
            copy.wait_recv()
            copy.start()

    def take(buf, send, recv):
        for k in range(lines):
            core_copy(buf, chip_at(k) * CORES + 1 - core, send, recv).wait_recv()

    pass_on(kv, core_send, kv_recv)

    @pl.when(is_host)
    def _():
        pass_on(kx, corex_send, kx_recv)

    take(kv, core_send, kv_recv)
    for k in range(1, WAYS):
        way_wait(k, qb, q_send, q_recv).wait_recv()

    step = n // blocks
    span = step * pad
    position = lax.broadcasted_iota(jnp.int32, (1, span), 1)
    padding = jnp.where(lax.rem(position, pad) < rows, 0.0, NEG)

    def bias_for(owner, b):
        start = (owner - b * step) * pad
        return jnp.where((position >= start) & (position < start + pad), NEG, padding)

    owners = [(block * WAYS + w) * CORES + core for w in range(WAYS)]

    def stale_part(packed, buf, dst):
        folds = packed[...].reshape(WAYS * fold, PAIR).astype(F32)
        query = jnp.concatenate(
            [jnp.where(half, folds, 0.0), jnp.where(half, swap(folds), 0.0)], axis=0
        ).astype(BF16)

        def one(b):
            pair = buf[pl.ds(b * step, step)].reshape(span, PAIR)
            biases = [bias_for(o, b) for o in owners]
            return one_head(query, pair, pair, biases + biases, fold)

        state = one(0)
        if blocks > 1:
            state = lax.fori_loop(1, blocks, lambda b, s: merge(s, one(b)), state)
        lse, part = state
        low, high = part[:WAYS * fold], part[WAYS * fold:]
        part = jnp.where(half, swap(high), low)
        lse = jnp.where(half, lse[WAYS * fold:], lse[:WAYS * fold])
        none = jnp.zeros((1, PAIR), F32)
        for w in range(WAYS):
            cut = slice(w * fold, (w + 1) * fold)
            flat = jnp.transpose(
                jnp.concatenate([lse[cut], jnp.zeros((PAIR - fold, PAIR), F32)], axis=0)
            )
            stats = jnp.concatenate(
                [*thirds(flat[0:1]), *thirds(flat[PAIR // 2:PAIR // 2 + 1]), none, none], axis=0
            )
            body = part[cut]
            end = jnp.where(half, stats, body[fold - 8:])
            dst[w] = jnp.concatenate([body[:fold - 8], end], axis=0).astype(BF16)

    stale_part(qb, kv, og)
    for k in range(1, WAYS):
        way_copy(k, og, ob, o_send, o_recv).start()
    ob[way] = og[way]

    @pl.when(is_host)
    def _():
        take(kx, corex_send, kx_recv)
        for k in range(1, WAYS):
            way_wait(k, qx, ox_send, qx_recv).wait_recv()
        stale_part(qx, kx, ox)
        for k in range(1, WAYS):
            host_result(k).start()
        ob[extra] = ox[way]

    def unfold(h):
        got = ob[h].astype(F32)
        stats = got[fold - 8:]
        high = stats[0:1] + stats[1:2] + stats[2:3]
        low = stats[3:4] + stats[4:5] + stats[5:6]
        lse = jnp.transpose(
            jnp.concatenate(
                [jnp.broadcast_to(high, (PAIR // 2, PAIR)), jnp.broadcast_to(low, (PAIR // 2, PAIR))],
                axis=0,
            )
        )[:fold]
        both = []
        for a in (lse, got):
            order = [swap(a), a] if h % 2 == 0 else [a, swap(a)]
            both.append(jnp.concatenate(order, axis=0))
        return both

    for k in range(1, WAYS):
        way_wait(k, ob, o_send, o_recv).wait_recv()
    heads = []
    for p in range(pairs):
        if p == WAYS // 2:
            for e in range(2):
                @pl.when(way != HOSTS[e])
                def _():
                    host_result_wait(e).wait_recv()
        even, odd = unfold(2 * p), unfold(2 * p + 1)
        stale = (jnp.where(half, even[0], odd[0]), jnp.where(half, even[1], odd[1]))
        heads.append(merge(fresh[p], stale)[1].astype(BF16))
    attended = jnp.concatenate(heads, axis=1)
    out_copy.wait()
    result = jnp.dot(attended, wo[...], preferred_element_type=F32) + bias_ref[...][None]
    out_ref[...] = result.astype(BF16)[:rows]

    for i in range(n - 1):
        mom_copy(i).wait_send()
    for e in range(2):
        for b in range(blocks):
            @pl.when(chip != b * WAYS + HOSTS[e])
            def _():
                host_copy(e, b).wait_send()

        @pl.when(way != HOSTS[e])
        def _():
            host_query(e).wait_send()
    for k in range(1, lines):
        line_copy(k).wait_send()
    for k in range(lines):
        core_copy(kv, chip_at(k) * CORES + core, core_send, kv_recv).wait_send()
    for k in range(1, WAYS):
        way_copy(k, qs, qb, q_send, q_recv).wait_send()
        way_copy(k, og, ob, o_send, o_recv).wait_send()

    @pl.when(is_host)
    def _():
        for k in range(lines):
            core_copy(kx, chip_at(k) * CORES + core, corex_send, kx_recv).wait_send()
        for k in range(1, WAYS):
            host_result(k).wait_send()


def solution(mesh):
    n = mesh.shape["patch"]

    def local(latents, stale_kv, stale_moments, norm_gain, norm_shift, w_qkv, w_out, out_bias):
        rows, width = latents.shape
        inner = w_out.shape[0]
        pad = -(-rows // 32) * 32
        heads = inner * 2 // PAIR
        chips = n // CORES
        vmem = pl.BlockSpec(memory_space=pltpu.VMEM)
        hbm = pl.BlockSpec(memory_space=pltpu.HBM)
        dma = pltpu.SemaphoreType.DMA
        return pl.pallas_call(
            functools.partial(kernel, n, rows, pad),
            out_shape=(
                jax.ShapeDtypeStruct((rows, w_out.shape[1]), BF16),
                jax.ShapeDtypeStruct((rows, 2 * inner), BF16),
            ),
            in_specs=[hbm] * 8,
            out_specs=(vmem, vmem),
            scratch_shapes=[
                pltpu.VMEM(latents.shape, BF16),
                pltpu.VMEM(stale_kv.shape, BF16),
                pltpu.VMEM(stale_moments.shape, F32),
                pltpu.VMEM(norm_gain.shape, F32),
                pltpu.VMEM(norm_shift.shape, F32),
                pltpu.VMEM(out_bias.shape, F32),
                pltpu.VMEM((heads, pad, PAIR), BF16),
                pltpu.VMEM((n, pad, PAIR), BF16),
                pltpu.VMEM((n, pad, PAIR), BF16),
                pltpu.VMEM((n, 8, stale_moments.shape[1]), F32),
                pltpu.VMEM((heads, pad // 2, PAIR), BF16),
                pltpu.VMEM((WAYS, pad // 2, PAIR), BF16),
                pltpu.VMEM((WAYS, pad // 2, PAIR), BF16),
                pltpu.VMEM((heads, pad // 2, PAIR), BF16),
                pltpu.VMEM((WAYS, pad // 2, PAIR), BF16),
                pltpu.VMEM((WAYS, pad // 2, PAIR), BF16),
                pltpu.VMEM((3, width, inner), BF16),
                pltpu.VMEM(w_out.shape, BF16),
                dma((n,)), dma((n,)), dma((chips,)), dma((n,)), dma((2 * chips // WAYS,)),
                dma((n,)), dma((n,)), dma((n,)),
                dma((WAYS,)), dma((WAYS,)), dma((2,)), dma((WAYS,)),
                dma((WAYS,)), dma((heads,)), dma((WAYS,)), dma((4,)), dma((6,)),
            ],
            compiler_params=pltpu.CompilerParams(
                collective_id=0, has_side_effects=True, vmem_limit_bytes=63 * 1024 * 1024
            ),
        )(
            latents, stale_kv, stale_moments, norm_gain, norm_shift, w_qkv, w_out, out_bias,
        )

    strip = P(("groups", "patch"), None)
    return jax.shard_map(
        local,
        mesh=mesh,
        in_specs=(strip, strip, strip, P(), P(), P(), P(), P()),
        out_specs=(strip, strip),
        check_vma=False,
    )
```

time: 39.6 us -> 34.4 us (0.87)
  local copies, waits for them, and re-layouts: 6.01 us -> 3.28 us
  Pallas kernels: 32.5 us -> 30.3 us
    pallas_call x1, Pallas kernels: 32.5 us -> 30.3 us  [local(): pl.pallas_call(functools.partial(kernel, n, rows, pad), out_shape=(jax.Sh...]
    broadcast_in_dim x3 -> x0, local copies, waits for them, and re-layouts: 2.1 us -> none  [the longest x1 0.7 us: local(): norm_gain[None]]
    unnamed x8 -> x2, local copies, waits for them, and re-layouts: 3.9 us -> 3.28 us
where the time goes in v2:
time: 34.4 us; the launch traced here: 34.2 us
  Pallas kernels  30.3 us (88%)
  local copies, waits for them, and re-layouts  3.28 us (10%)
  between operations  0.64 us (2%)
    pallas_call x1, Pallas kernels, local(): pl.pallas_call(functools.partial(kernel, n, rows, pad), out_shape=(jax.Sh...  30.3 us
    unnamed x2, local copies, waits for them, and re-layouts  3.28 us

profile of v2, /device:TPU:0, one launch (start us, length us, event | category | flops | bytes accessed | tf_op | source)
XLA Modules:
  0.0 34.2 jit_solution(1751344936156358850)
XLA Ops:
  0.6 30.3 %shard_map.95 = (bf16[88,1280]{1,0:T(8,128)(2,1)}, bf16[88,1280]{1,0:T(8,128)(2,1)}) custom-call(bf16[88,1280]{1,0:T(8,128)(2,1)} %x_hbm.1, bf16[88,1280]{1,0:T(8,128)(2,1)} %stale_hbm.1, f32[1,64]{1,0:T(1,128)} %mom_hbm.1, f32[1280]{0:T(1024)} %gain_hbm.1, f32[1280]{0:T(1024)} %shift_hbm.1, bf16[1280,1920]{1,0:T(8,128)(2,1)} %wqkv_ref.1, ...), custom_call_target="tpu_custom_call" | custom-call | tf_op jit(solution)/shard_map/pallas_call | solution.py:459
  30.9 1.6 %copy.12 = bf16[88,1280]{1,0:T(8,128)(2,1)} copy(bf16[88,1280]{1,0:T(8,128)(2,1)} %get-tuple-element.4) | data formatting | bytes 450560
  32.5 1.6 %copy.13 = bf16[88,1280]{1,0:T(8,128)(2,1)} copy(bf16[88,1280]{1,0:T(8,128)(2,1)} %get-tuple-element.5) | data formatting | bytes 450560

commit v3 on v2

--- a/solution.py
+++ b/solution.py
@@ -299,28 +299,29 @@
         mass = wa + wb
         return top + jnp.log(mass), (wa * a[1] + wb * b[1]) / mass
 
+    def pass_on(buf, send, recv, steps):
+        for k in steps:
+            copy = core_copy(buf, chip_at(k) * CORES + core, send, recv)
+            copy.wait_recv()
+            copy.start()
+
     key_lane = lax.broadcasted_iota(jnp.int32, (1, pad), 1)
     own_bias = jnp.where(key_lane < rows, 0.0, NEG)
     fresh = []
+    order = sorted(range(1, lines), key=lambda k: min(k, lines - k))
+    share = -(-len(order) // pairs)
     for p in range(pairs):
         cut = slice(p * PAIR, (p + 1) * PAIR)
         fresh.append(attend(queries[:, cut], keys[:, cut], values[:, cut], [own_bias]))
-
-    def pass_on(buf, send, recv):
-        for k in range(1, lines):
-            copy = core_copy(buf, chip_at(k) * CORES + core, send, recv)
-            copy.wait_recv()
-            copy.start()
+        pass_on(kv, core_send, kv_recv, order[p * share:(p + 1) * share])
 
     def take(buf, send, recv):
         for k in range(lines):
             core_copy(buf, chip_at(k) * CORES + 1 - core, send, recv).wait_recv()
 
-    pass_on(kv, core_send, kv_recv)
-
     @pl.when(is_host)
     def _():
-        pass_on(kx, corex_send, kx_recv)
+        pass_on(kx, corex_send, kx_recv, range(1, lines))
 
     take(kv, core_send, kv_recv)
     for k in range(1, WAYS):

time: 34.4 us -> 34.3 us (level)
  no operation moved by 1% of the time
where the time goes in v3:
time: 34.3 us; the launch traced here: 34.2 us
  Pallas kernels  30.3 us (88%)
  local copies, waits for them, and re-layouts  3.28 us (10%)
  between operations  0.64 us (2%)
    pallas_call x1, Pallas kernels, local(): pl.pallas_call(functools.partial(kernel, n, rows, pad), out_shape=(jax.Sh...  30.3 us
    unnamed x2, local copies, waits for them, and re-layouts  3.28 us

profile of v3, /device:TPU:0, one launch (start us, length us, event | category | flops | bytes accessed | tf_op | source)
XLA Modules:
  0.0 34.2 jit_solution(5779129276725072924)
XLA Ops:
  0.6 30.3 %shard_map.95 = (bf16[88,1280]{1,0:T(8,128)(2,1)}, bf16[88,1280]{1,0:T(8,128)(2,1)}) custom-call(bf16[88,1280]{1,0:T(8,128)(2,1)} %x_hbm.1, bf16[88,1280]{1,0:T(8,128)(2,1)} %stale_hbm.1, f32[1,64]{1,0:T(1,128)} %mom_hbm.1, f32[1280]{0:T(1024)} %gain_hbm.1, f32[1280]{0:T(1024)} %shift_hbm.1, bf16[1280,1920]{1,0:T(8,128)(2,1)} %wqkv_ref.1, ...), custom_call_target="tpu_custom_call" | custom-call | tf_op jit(solution)/shard_map/pallas_call | solution.py:460
  30.9 1.6 %copy.12 = bf16[88,1280]{1,0:T(8,128)(2,1)} copy(bf16[88,1280]{1,0:T(8,128)(2,1)} %get-tuple-element.4) | data formatting | bytes 450560
  32.5 1.6 %copy.13 = bf16[88,1280]{1,0:T(8,128)(2,1)} copy(bf16[88,1280]{1,0:T(8,128)(2,1)} %get-tuple-element.5) | data formatting | bytes 450560
